TPU v7x, 768 devices: a whole 4x8x12 slice. The times are simulated.
768 devices in a mesh: rows: 32 (over x, y), groups: 24 (over z, core).
Axes of the slice: x: 4, y: 8, z: 12, core: 2. Of those that a mesh axis runs over, the one named last changes fastest.
Arguments:
- next_owner: int32 [98304, 16, 1], P(('rows', 'groups')), may hold values from 0 to 31; in each aligned block of 2048 rows (0 to 2047, 2048 to 4095, ..., all dimensions but the last counted through in order) at most 96 rows name the same one
- next_row: int32 [98304, 16], P(('rows', 'groups')), may hold values from 0 to 767
- prev_owner: int32 [98304, 16, 1], P(('rows', 'groups')), may hold values from 0 to 31; in each aligned block of 2048 rows (0 to 2047, 2048 to 4095, ..., all dimensions but the last counted through in order) at most 96 rows name the same one
- prev_row: int32 [98304, 16], P(('rows', 'groups')), may hold values from 0 to 767
- emb_now: bfloat16 [98304, 4096], P(('rows', 'groups')), may hold values from -6 to 6
- prev_grad: bfloat16 [98304, 4096], P(('rows', 'groups')), may hold values from -6 to 6
- labels: int32 [98304], P(('rows', 'groups')), may hold values 0 or 1
- emb_table: float32 [24576, 256], P('rows'), may hold values from -6 to 6
- row_accum: float32 [24576], P('rows'), may hold values from 0.1 to 10
- proj_in: bfloat16 [128, 4096], replicated, may hold values from -0.09375 to 0.09375
- proj_out: bfloat16 [128, 4096], replicated, may hold values from -0.5 to 0.5
- cross_bias: float32 [4096], replicated, may hold values from -3 to 3
- head_weight: bfloat16 [4096], replicated, may hold values from -0.09375 to 0.09375
Outputs:
- next_emb: bfloat16 [98304, 4096], P(('rows', 'groups'))
- emb_grad: bfloat16 [98304, 4096], P(('rows', 'groups'))
- new_table: float32 [24576, 256], P('rows')
- new_accum: float32 [24576], P('rows')
- grad_in: float32 [128, 4096], P(None, 'rows')
- grad_out: float32 [128, 4096], P(None, 'rows')
- grad_bias: float32 [4096], P('rows')
- grad_head: float32 [4096], P('rows')
Inputs may be any that keep to these rules, and one draw needn't show every extreme that they name: `next_owner`: at most 96 of the 2048 lookups of one device's samples name rows held by one device of the rows axis, and exactly 96 for some devices. `prev_owner`: at most 96 of the 2048 lookups of one device's samples name rows held by one device of the rows axis, and exactly 96 for some devices.
All inputs are finite; a program needn't handle non-finite values. No bound on the sum of `labels` on one device may be relied on, other than what follows from the above.
Results may differ from a plain program's by a relative error of at most 0.0059.
Values may be sent and summed in bfloat16 or wider, within the bound.
A program may use at most 64 MiB of HBM per device.

v0:
```python
import math

import jax
import jax.numpy as jnp
from jax import lax
from jax.sharding import PartitionSpec as P

LEARN_RATE = 0.1
EPSILON = 1e-06
LOSS_SCALE = 64.0


def slot_ranks(owners, peer_count):
    onehot = (owners[:, None] == jnp.arange(peer_count, dtype=jnp.int32)[None, :]).astype(jnp.int32)
    before = jnp.cumsum(onehot, axis=0) - onehot
    return jnp.sum(before * onehot, axis=1)


def shards(
    next_owner,
    next_row,
    prev_owner,
    prev_row,
    emb_now,
    prev_grad,
    labels,
    emb_table,
    row_accum,
    proj_in,
    proj_out,
    cross_bias,
    head_weight,
):
    peer_count = lax.axis_size("rows")
    samples = emb_now.shape[0]
    row_width = emb_table.shape[1]
    shard_rows = emb_table.shape[0]
    lookups = next_owner.shape[0] * next_owner.shape[1]
    capacity = 3 * lookups // (2 * peer_count)
    batch_total = samples * peer_count * lax.axis_size("groups")
    next_dest = next_owner.reshape(lookups)
    prev_dest = prev_owner.reshape(lookups)
    next_slot = slot_ranks(next_dest, peer_count)
    prev_slot = slot_ranks(prev_dest, peer_count)
    empty_ids = jnp.full((peer_count, capacity), shard_rows, jnp.int32)
    next_asks = empty_ids.at[next_dest, next_slot].set(next_row.reshape(lookups))
    prev_asks = empty_ids.at[prev_dest, prev_slot].set(prev_row.reshape(lookups))
    outgoing = (
        jnp.zeros((peer_count, capacity, row_width), jnp.bfloat16)
        .at[prev_dest, prev_slot]
        .set(prev_grad.reshape(lookups, row_width))
    )
    table_half = emb_table.astype(jnp.bfloat16)
    asked_rows = lax.all_to_all(next_asks, "rows", split_axis=0, concat_axis=0, tiled=True)
    prev_asked = lax.all_to_all(prev_asks, "rows", split_axis=0, concat_axis=0, tiled=True)
    fetched = table_half[jnp.minimum(asked_rows, shard_rows - 1)]
    looked = lax.all_to_all(fetched, "rows", split_axis=0, concat_axis=0, tiled=True)
    next_emb = looked[next_dest, next_slot].reshape(samples, -1)
    arrived = lax.all_to_all(outgoing, "rows", split_axis=0, concat_axis=0, tiled=True)
    shard_grad = (
        jnp.zeros((shard_rows, row_width), jnp.float32)
        .at[prev_asked.reshape(-1)]
        .add(arrived.reshape(-1, row_width).astype(jnp.float32), mode="drop")
    )
    row_sums = lax.psum(shard_grad.astype(jnp.bfloat16), "groups").astype(jnp.float32)
    head_float = head_weight.astype(jnp.float32)
    latent = lax.dot_general(
        emb_now, proj_in, (((1,), (1,)), ((), ())), preferred_element_type=jnp.float32
    ).astype(jnp.bfloat16)
    cross_gate = jnp.dot(latent, proj_out, preferred_element_type=jnp.float32) + cross_bias
    inputs = emb_now.astype(jnp.float32)
    crossed = inputs * cross_gate + inputs
    logits = jnp.sum(crossed * head_float[None, :], axis=1)
    errors = LOSS_SCALE * (jax.nn.sigmoid(logits) - labels.astype(jnp.float32))
    grad_crossed = errors[:, None] * head_float[None, :]
    grad_gate = (grad_crossed * inputs).astype(jnp.bfloat16)
    grad_latent = lax.dot_general(
        grad_gate, proj_out, (((1,), (1,)), ((), ())), preferred_element_type=jnp.float32
    ).astype(jnp.bfloat16)
    emb_grad = (
        grad_crossed * (cross_gate + 1.0)
        + jnp.dot(grad_latent, proj_in, preferred_element_type=jnp.float32)
    ).astype(jnp.bfloat16)
    grad_in = lax.dot_general(
        grad_latent, emb_now, (((0,), (0,)), ((), ())), preferred_element_type=jnp.float32
    )
    grad_out = lax.dot_general(
        latent, grad_gate, (((0,), (0,)), ((), ())), preferred_element_type=jnp.float32
    )
    grad_bias = jnp.sum(grad_gate.astype(jnp.float32), axis=0)
    grad_head = jnp.sum(errors[:, None] * crossed, axis=0)
    vectors = jnp.stack([grad_bias, grad_head], axis=0)
    slices = (
        lax.psum_scatter(grad_in, "rows", scatter_dimension=1, tiled=True),
        lax.psum_scatter(grad_out, "rows", scatter_dimension=1, tiled=True),
        lax.psum_scatter(vectors, "rows", scatter_dimension=1, tiled=True),
    )
    totals = lax.psum((slices[0], slices[1], slices[2]), "groups")
    factor = 1.0 / math.sqrt(batch_total)
    new_accum = row_accum + jnp.mean(row_sums * row_sums, axis=1)
    new_table = emb_table - LEARN_RATE * row_sums / (jnp.sqrt(new_accum)[:, None] + EPSILON)
    return (
        next_emb,
        emb_grad,
        new_table,
        new_accum,
        totals[0] * factor,
        totals[1] * factor,
        totals[2][0] * factor,
        totals[2][1] * factor,
    )


def solution(mesh):
    placed = (
        P(("rows", "groups"), None, None),
        P(("rows", "groups"), None),
        P(("rows", "groups"), None, None),
        P(("rows", "groups"), None),
        P(("rows", "groups"), None),
        P(("rows", "groups"), None),
        P(("rows", "groups")),
        P("rows", None),
        P("rows"),
        P(),
        P(),
        P(),
        P(),
    )
    return jax.shard_map(
        shards,
        mesh=mesh,
        in_specs=placed,
        out_specs=(
            P(("rows", "groups"), None),
            P(("rows", "groups"), None),
            P("rows", None),
            P("rows"),
            P(None, "rows"),
            P(None, "rows"),
            P("rows"),
            P("rows"),
        ),
        check_vma=False,
    )
```

profile of v0, /device:TPU:1, one launch (start us, length us, event | category | flops | bytes accessed | tf_op | source)
XLA Modules:
  0.0 1020.5 jit_solution(2868668665215827688)
XLA Ops:
  8.0 0.9 copy.33
  9.2 0.8 copy.39
  10.2 0.8 copy.44
  11.2 9.1 reduce-window.16
  20.3 9.1 reduce-window.14
  29.5 0.2 copy.45
  29.7 0.2 reduce-window.15
  30.2 0.2 copy.46
  30.4 0.2 reduce-window.19
  31.4 8.1 scatter_custom_fusion.2
  39.4 0.7 all_to_all.21
  40.1 10.5 %all-to-all-start.2 = ((s32[32,1,96]{2,1,0:T(1,128)}), s32[32,1,96]{2,1,0:T(1,128)S(1)}, u32[]{:S(2)}, u32[]{:S(2)}) async-start(s32[32,1,96]{2,1,0:T(1,128)} %all_to_all.21), calls=%async_computation.2 | async-start | bytes 32768 | tf_op jit(solution)/shard_map/all_to_all | solution.py:55
  50.6 1.3 reshape.279
  52.0 11.1 %scatter_custom_fusion.3 = bf16[3072,256]{1,0:T(8,128)(2,1)} fusion(s32[2048]{0:T(1024)S(1)} %get-tuple-element.27, bf16[2048,256]{1,0:T(8,128)(2,1)} %reshape.279, bf16[]{:T(256)} %constant.6.clone.1), kind=kCustom, calls=%fused_computation.25 | custom fusion | bytes 1573376
  63.1 9.5 all-to-all-start.3
  72.6 0.4 convolution_convert_fusion.1
  73.1 0.7 multiply_reduce_fusion.1
  73.9 1.3 copy-done.2
  75.2 0.7 convert_reduce_fusion
  75.9 0.5 broadcast.249
  76.4 0.7 reduce.13
  77.2 26.3 %all-to-all-done.3 = bf16[32,96,256]{2,1,0:T(8,128)(2,1)} async-done(((bf16[32,96,256]{2,1,0:T(8,128)(2,1)}), bf16[32,96,256]{2,1,0:T(8,128)(2,1)}, u32[]{:S(2)}, u32[]{:S(2)}) %all-to-all-start.3) | async-done | bytes 1572896 | tf_op jit(solution)/shard_map/all_to_all | solution.py:59
  103.5 16.1 %scatter_custom_fusion = f32[768,256]{1,0:T(8,128)S(1)} fusion(s32[3072]{0:T(1024)S(1)} %bitcast.100, bf16[3072,256]{1,0:T(8,128)(2,1)} %bitcast.20, f32[]{:T(128)} %constant.19.clone.1), kind=kCustom, calls=%fused_computation.9 | custom fusion | flops 1572864 | bytes 2359300 | tf_op jit(solution)/shard_map/scatter-add | solution.py:63
  119.7 0.8 convert_element_type.67
  120.6 2.0 copy.47
  122.6 0.2 reduce-scatter.8.cloned.1.call-start
  122.8 1.8 fusion.23
  124.7 0.5 convolution_convert_fusion
  125.2 1.8 fusion.26
  127.3 8.1 scatter_custom_fusion.1
  135.4 18.0 %all_to_all.28 = s32[32,1,96]{2,1,0:T(1,128)S(1)} all-to-all(s32[32,1,96]{2,1,0:T(1,128)S(1)} %all_to_all.18), channel_id=1, replica_groups=mesh['rows'=32,'groups'=24] {'rows'}, dimensions={0} | all-to-all | bytes 24576 | tf_op jit(solution)/shard_map/all_to_all | solution.py:54
  153.6 144.3 %all-reduce.4.cloned.1.call-done = bf16[768,256]{1,0:T(8,128)(2,1)} async-done(((bf16[768,256]{1,0:T(8,128)(2,1)}), bf16[768,256]{1,0:T(8,128)(2,1)}) %all-reduce.4.cloned.1.call-update) | async-done | bytes 393232 | tf_op jit(solution)/shard_map/psum | solution.py:65
  297.9 1.2 fusion.6
  299.0 0.6 sqrt_add_fusion
  299.6 2.1 fusion.5
  301.7 13.0 %gather_fusion = bf16[3072,256]{1,0:T(8,128)(2,1)} fusion(bf16[768,256]{1,0:T(8,128)(2,1)S(1)} %get-tuple-element.19, s32[3072]{0:T(1024)S(1)} %broadcast_clamp_fusion), kind=kCustom, calls=%fused_computation | custom fusion | bytes 3158016 | tf_op jit(solution)/shard_map/gather | solution.py:56
  314.7 9.5 all-to-all-start.1
  324.2 3.4 fusion
  327.6 37.8 %reduce-scatter.10.cloned.1.call-done = f32[128,2]{1,0:T(8,128)} async-done(((f32[4096,2]{1,0:T(8,128)}), f32[128,2]{1,0:T(8,128)}) %reduce-scatter.10.cloned.1.call-update) | async-done | bytes 1040
  365.4 0.9 copy.48
  366.3 40.1 %psum.31 = f32[2,128]{1,0:T(2,128)S(1)} all-reduce(f32[2,128]{1,0:T(2,128)S(1)} %copy.48), channel_id=1, replica_groups=mesh['rows'=32,'groups'=24] {'groups'}, use_global_device_ids=true, to_apply=%region_20.21 | all-reduce | flops 256 | bytes 2048 | tf_op jit(solution)/shard_map/psum | solution.py:98
  406.4 188.6 %reduce-scatter.8.cloned.1.call-done = f32[128,128]{1,0:T(8,128)} async-done(((f32[128,4096]{1,0:T(8,128)}), f32[128,128]{1,0:T(8,128)}) %reduce-scatter.8.cloned.1.call-update) | async-done | bytes 65552 | tf_op jit(solution)/shard_map/reduce_scatter | solution.py:95
  595.0 232.6 %reduce-scatter.6.cloned.1.call-done = f32[128,128]{1,0:T(8,128)} async-done(((f32[128,4096]{1,0:T(8,128)}), f32[128,128]{1,0:T(8,128)}) %reduce-scatter.6.cloned.1.call-update) | async-done | bytes 65552 | tf_op jit(solution)/shard_map/reduce_scatter | solution.py:94
  827.6 0.5 multiply_bitcast_fusion
  828.1 160.2 %all-reduce.6.cloned.1.call-done = (f32[128,128]{1,0:T(8,128)}, f32[128,128]{1,0:T(8,128)}) async-done(((f32[128,128]{1,0:T(8,128)}, f32[128,128]{1,0:T(8,128)}), (f32[128,128]{1,0:T(8,128)}, f32[128,128]{1,0:T(8,128)})) %all-reduce.6.cloned.1.call-update) | async-done | bytes 131088 | tf_op jit(solution)/shard_map/psum | solution.py:98
  988.3 1.5 broadcast_multiply_fusion
  989.9 20.7 %gather_fusion.1 = bf16[2048,256]{1,0:T(8,128)(2,1)} fusion(bf16[32,96,256]{2,1,0:T(8,128)(2,1)S(1)} %all-to-all-done.1, s32[2048]{0:T(1024)S(1)} %bitcast.84), kind=kCustom, calls=%fused_computation.1 | custom fusion | bytes 2113536 | tf_op jit(solution)/shard_map/gather | solution.py:58
  1010.6 2.3 reshape.222
  (69 shorter events, 2.5 us)
Async XLA Ops:
  8.0 65.1 %copy-start = (bf16[128,4096]{1,0:T(8,128)(2,1)S(1)}, bf16[128,4096]{1,0:T(8,128)(2,1)}, u32[]{:S(2)}) copy-start(bf16[128,4096]{1,0:T(8,128)(2,1)} %param.23) | copy-start | bytes 3145732
  11.2 19.9 %copy-start.11 = (s32[2]{0:T(128)S(1)}, s32[2]{0:T(128)}, u32[]{:S(2)}) copy-start(s32[2]{0:T(128)} %constant.50) | copy-start | bytes 28
  20.3 11.0 %copy-start.10 = (s32[2]{0:T(128)S(1)}, s32[2]{0:T(128)}, u32[]{:S(2)}) copy-start(s32[2]{0:T(128)} %constant.47) | copy-start | bytes 28
  20.3 30.4 %copy-start.4 = (bf16[128,4096]{1,0:T(8,128)(2,1)S(1)}, bf16[128,4096]{1,0:T(8,128)(2,1)}, u32[]{:S(2)}) copy-start(bf16[128,4096]{1,0:T(8,128)(2,1)} %param.18) | copy-start | bytes 3145732
  40.1 22.9 %all-to-all-start.2 = ((s32[32,1,96]{2,1,0:T(1,128)}), s32[32,1,96]{2,1,0:T(1,128)S(1)}, u32[]{:S(2)}, u32[]{:S(2)}) async-start(s32[32,1,96]{2,1,0:T(1,128)} %all_to_all.21), calls=%async_computation.2 | async-start | bytes 32768 | tf_op jit(solution)/shard_map/all_to_all | solution.py:55
  51.9 20.6 %copy-start.7 = (bf16[4096]{0:T(1024)(128)(2,1)S(1)}, bf16[4096]{0:T(1024)(128)(2,1)}, u32[]{:S(2)}) copy-start(bf16[4096]{0:T(1024)(128)(2,1)} %param.25) | copy-start | bytes 24580
  52.0 20.7 %copy-start.1 = (bf16[128,4096]{1,0:T(8,128)(2,1)S(1)}, bf16[128,4096]{1,0:T(8,128)(2,1)}, u32[]{:S(2)}) copy-start(bf16[128,4096]{1,0:T(8,128)(2,1)} %param.17) | copy-start | bytes 3145732
  52.0 20.7 %copy-start.3 = (bf16[128,4096]{1,0:T(8,128)(2,1)S(1)}, bf16[128,4096]{1,0:T(8,128)(2,1)}, u32[]{:S(2)}) copy-start(bf16[128,4096]{1,0:T(8,128)(2,1)} %param.22) | copy-start | bytes 3145732
  63.1 10.0 copy-start.6
  63.1 40.5 %all-to-all-start.3 = ((bf16[32,96,256]{2,1,0:T(8,128)(2,1)}), bf16[32,96,256]{2,1,0:T(8,128)(2,1)}, u32[]{:S(2)}, u32[]{:S(2)}) async-start(bf16[32,96,256]{2,1,0:T(8,128)(2,1)} %bitcast.86), calls=%async_computation.3 | async-start | bytes 3145728 | tf_op jit(solution)/shard_map/all_to_all | solution.py:59
  72.5 225.3 %all-reduce.4.cloned.1.call-start = ((), (), s32[]{:S(2)}) async-start(), calls=%async_computation.7 | async-start | bytes 786432 | tf_op jit(solution)/shard_map/psum | solution.py:65
  73.1 0.8 copy-start.12
  73.9 1.4 copy-start.2
  120.5 244.9 %reduce-scatter.10.cloned.1.call-start = ((), (), s32[]{:S(2)}) async-start(), calls=%async_computation.10 | async-start | bytes 2162688
  122.6 472.4 %reduce-scatter.8.cloned.1.call-start = ((), (), s32[]{:S(2)}) async-start(), calls=%async_computation.9 | async-start | bytes 2162688 | tf_op jit(solution)/shard_map/reduce_scatter | solution.py:95
  124.7 702.9 %reduce-scatter.6.cloned.1.call-start = ((), (), s32[]{:S(2)}) async-start(), calls=%async_computation.8 | async-start | bytes 2162688 | tf_op jit(solution)/shard_map/reduce_scatter | solution.py:94
  125.2 1.8 copy-start.8
  127.0 172.0 %copy-start.9 = (f32[768]{0:T(1024)S(1)}, f32[768]{0:T(1024)}, u32[]{:S(2)}) copy-start(f32[768]{0:T(1024)} %param.21) | copy-start | bytes 9220
  127.0 172.6 %copy-start.5 = (f32[768,256]{1,0:T(8,128)S(1)}, f32[768,256]{1,0:T(8,128)}, u32[]{:S(2)}) copy-start(f32[768,256]{1,0:T(8,128)} %param.20) | copy-start | bytes 2359300
  314.7 675.2 %all-to-all-start.1 = ((bf16[32,96,256]{2,1,0:T(8,128)(2,1)}), bf16[32,96,256]{2,1,0:T(8,128)(2,1)S(1)}, u32[]{:S(2)}, u32[]{:S(2)}) async-start(bf16[32,96,256]{2,1,0:T(8,128)(2,1)} %bitcast.87), calls=%async_computation.1 | async-start | bytes 3145728 | tf_op jit(solution)/shard_map/all_to_all | solution.py:57
  324.2 664.2 %all-reduce.6.cloned.1.call-start = ((), (), s32[]{:S(2)}) async-start(), calls=%async_computation.11 | async-start | bytes 262144 | tf_op jit(solution)/shard_map/psum | solution.py:98
Sparse Core Ops, SparseCore 0:
  120.6 177.2 all-reduce.3
  827.7 160.5 all-reduce.5
Sparse Core Ops, SparseCore 1:
  126.7 238.6 reduce-scatter.9
  370.3 224.7 reduce-scatter.7
  600.6 226.9 reduce-scatter.5
where the time goes:
time: 1020 us
  waiting for transfers between devices  790 us (77%)
  local copies, waits for them, and re-layouts  74.2 us (7%)
  blocking collectives  58.2 us (6%)
  other arithmetic  43.6 us (4%)
  starting transfers between devices  29.8 us (3%)
  between operations  16.1 us (2%)
    reduce_scatter x1, waiting for transfers between devices, shards(): lax.psum_scatter(grad_in, 'rows', scatter_dimension=1, tiled=True)  233 us
    reduce_scatter x1, waiting for transfers between devices, shards(): lax.psum_scatter(grad_out, 'rows', scatter_dimension=1, tiled=True)  189 us
    psum x1, waiting for transfers between devices, shards(): totals = lax.psum((slices[0], slices[1], slices[2]), 'groups')  160 us
    psum x1, waiting for transfers between devices, shards(): lax.psum(shard_grad.astype(jnp.bfloat16), 'groups').astype(jnp.float32)  144 us
    psum x1, blocking collectives, shards(): totals = lax.psum((slices[0], slices[1], slices[2]), 'groups')  40.1 us
    unnamed x6, waiting for transfers between devices  37.9 us
    unnamed x35, local copies, waits for them, and re-layouts  34.1 us
    all_to_all x1, waiting for transfers between devices, shards(): lax.all_to_all(outgoing, 'rows', split_axis=0, concat_axis=0, tiled=True)  26.3 us
  transfers between devices with their start and end apart: 8, of which 6 were waited for; matrix products, arithmetic and copies ran while one was open for 5% of the time, Pallas kernels for 0%

commit v1 on v0

v1 whole, which is shorter than its diff:
```python
import math

import jax
import jax.numpy as jnp
from jax import lax
from jax.sharding import PartitionSpec as P

LEARN_RATE = 0.1
EPSILON = 1e-06
LOSS_SCALE = 64.0


def slot_keys(owners, peer_count, capacity):
    blocks, width = owners.shape
    onehot = (owners[:, :, None] == jnp.arange(peer_count, dtype=jnp.int32)).astype(jnp.bfloat16)
    earlier = jnp.tril(jnp.ones((width, width), jnp.bfloat16), -1)
    within = jnp.einsum("ij,bjp->bip", earlier, onehot, preferred_element_type=jnp.float32)
    totals = jnp.sum(onehot.astype(jnp.float32), axis=1)
    offsets = jnp.cumsum(totals, axis=0) - totals
    ranks = jnp.sum((within + offsets[:, None, :]) * onehot.astype(jnp.float32), axis=2)
    return owners * capacity + ranks.astype(jnp.int32)


def exchange(values, axis):
    return lax.all_to_all(values, axis, split_axis=0, concat_axis=0, tiled=True)


def shards(
    next_owner,
    next_row,
    prev_owner,
    prev_row,
    emb_now,
    prev_grad,
    labels,
    emb_table,
    row_accum,
    proj_in,
    proj_out,
    cross_bias,
    head_weight,
):
    peers = lax.axis_size("rows")
    copies = lax.axis_size("groups")
    samples, columns = emb_now.shape
    shard_rows, row_width = emb_table.shape
    features = next_owner.shape[1]
    lookups = samples * features
    capacity = 3 * lookups // (2 * peers)
    slots = peers * capacity
    rank = proj_in.shape[0]
    part = columns // peers
    batch_total = samples * peers * copies
    half = jnp.bfloat16
    full = jnp.float32

    next_key = slot_keys(next_owner[:, :, 0].T, peers, capacity)
    prev_key = slot_keys(prev_owner[:, :, 0].T, peers, capacity)
    slot_ids = jnp.arange(slots, dtype=jnp.int32)
    next_pick = (slot_ids[:, None] == next_key.reshape(1, lookups)).astype(half)
    prev_pick = (slot_ids[:, None] == prev_key.reshape(1, lookups)).astype(half)

    def asks(pick, rows):
        flat = rows.T.reshape(lookups) + 1
        digits = jnp.stack([flat // 32, flat % 32], axis=1).astype(half)
        found = jnp.dot(pick, digits, preferred_element_type=full)
        return (found[:, 0] * 32 + found[:, 1]).astype(jnp.int32) - 1

    asked = exchange(
        jnp.concatenate(
            [asks(next_pick, next_row).reshape(peers, capacity), asks(prev_pick, prev_row).reshape(peers, capacity)],
            axis=1,
        ),
        "rows",
    )
    next_asked = asked[:, :capacity].reshape(slots)
    prev_asked = asked[:, capacity:].reshape(slots)
    grads = prev_grad.reshape(samples, features, row_width).transpose(1, 0, 2).reshape(lookups, row_width)
    outgoing = jnp.dot(prev_pick, grads, preferred_element_type=full).astype(half)
    arrived = exchange(outgoing.reshape(peers, capacity, row_width), "rows").reshape(slots, row_width)

    head_float = head_weight.astype(full)
    latent = lax.dot_general(emb_now, proj_in, (((1,), (1,)), ((), ())), preferred_element_type=full).astype(half)
    cross_gate = jnp.dot(latent, proj_out, preferred_element_type=full) + cross_bias
    inputs = emb_now.astype(full)
    crossed = inputs * cross_gate + inputs
    logits = jnp.sum(crossed * head_float[None, :], axis=1)
    errors = LOSS_SCALE * (jax.nn.sigmoid(logits) - labels.astype(full))
    grad_crossed = errors[:, None] * head_float[None, :]
    grad_gate = (grad_crossed * inputs).astype(half)
    grad_latent = lax.dot_general(
        grad_gate, proj_out, (((1,), (1,)), ((), ())), preferred_element_type=full
    ).astype(half)
    emb_grad = (
        grad_crossed * (cross_gate + 1.0) + jnp.dot(grad_latent, proj_in, preferred_element_type=full)
    ).astype(half)
    grad_in = lax.dot_general(grad_latent, emb_now, (((0,), (0,)), ((), ())), preferred_element_type=full)
    grad_out = lax.dot_general(latent, grad_gate, (((0,), (0,)), ((), ())), preferred_element_type=full)
    grad_bias = jnp.sum(grad_gate.astype(full), axis=0)
    grad_head = jnp.sum(errors[:, None] * crossed, axis=0)
    dense_rows = 2 * rank + 2
    padded = -(-dense_rows // (2 * copies)) * 2 * copies
    dense = jnp.concatenate(
        [grad_in, grad_out, grad_bias[None], grad_head[None], jnp.zeros((padded - dense_rows, columns), full)], axis=0
    ).astype(half)
    dense = dense.reshape(padded, peers, part).transpose(1, 0, 2)
    dense = jnp.sum(exchange(dense, "rows").astype(full), axis=0)

    table_half = emb_table.astype(half)
    row_ids = jnp.arange(shard_rows, dtype=jnp.int32)
    fetched = jnp.dot(
        (next_asked[:, None] == row_ids[None, :]).astype(half), table_half, preferred_element_type=full
    ).astype(half)
    looked = exchange(fetched.reshape(peers, capacity, row_width), "rows").reshape(slots, row_width)
    next_emb = lax.dot_general(
        next_pick, looked, (((0,), (0,)), ((), ())), preferred_element_type=full
    ).astype(half)
    next_emb = next_emb.reshape(features, samples, row_width).transpose(1, 0, 2).reshape(samples, columns)

    shard_grad = jnp.dot(
        (row_ids[:, None] == prev_asked[None, :]).astype(half), arrived, preferred_element_type=full
    )
    share = shard_rows // copies
    pieces = jnp.concatenate(
        [
            shard_grad.reshape(copies, share, row_width),
            dense.reshape(copies, padded // (2 * copies), 2 * part),
        ],
        axis=1,
    ).astype(half)
    mine = jnp.sum(exchange(pieces, "groups").astype(full), axis=0).astype(half)
    whole = exchange(jnp.broadcast_to(mine[None], (copies,) + mine.shape), "groups").astype(full)
    row_sums = whole[:, :share].reshape(shard_rows, row_width)
    totals = whole[:, share:].reshape(padded, part) * (1.0 / math.sqrt(batch_total))
    new_accum = row_accum + jnp.mean(row_sums * row_sums, axis=1)
    new_table = emb_table - LEARN_RATE * row_sums / (jnp.sqrt(new_accum)[:, None] + EPSILON)
    return (
        next_emb,
        emb_grad,
        new_table,
        new_accum,
        totals[:rank],
        totals[rank : 2 * rank],
        totals[2 * rank],
        totals[2 * rank + 1],
    )


def solution(mesh):
    placed = (
        P(("rows", "groups"), None, None),
        P(("rows", "groups"), None),
        P(("rows", "groups"), None, None),
        P(("rows", "groups"), None),
        P(("rows", "groups"), None),
        P(("rows", "groups"), None),
        P(("rows", "groups")),
        P("rows", None),
        P("rows"),
        P(),
        P(),
        P(),
        P(),
    )
    return jax.shard_map(
        shards,
        mesh=mesh,
        in_specs=placed,
        out_specs=(
            P(("rows", "groups"), None),
            P(("rows", "groups"), None),
            P("rows", None),
            P("rows"),
            P(None, "rows"),
            P(None, "rows"),
            P("rows"),
            P("rows"),
        ),
        check_vma=False,
    )
```

time: 1020 us -> 262 us (0.26)
  waiting for transfers between devices: 790 us -> 129 us
  blocking collectives: 58.2 us -> 0 us
  local copies, waits for them, and re-layouts: 74.2 us -> 16.5 us
  starting transfers between devices: 29.8 us -> 67.5 us
  other arithmetic: 43.6 us -> 10.6 us
  matrix products: 8.73 us -> 35.7 us
  between operations: 16.1 us -> 1.07 us
    reduce_scatter x2 -> x0, waiting for transfers between devices: 421 us -> none  [the longest x1 233 us: shards(): lax.psum_scatter(grad_in, 'rows', scatter_dimension=1, tiled=True)]
    psum x2 -> x0, waiting for transfers between devices: 304 us -> none  [the longest x1 160 us: shards(): totals = lax.psum((slices[0], slices[1], slices[2]), 'groups')]
    all_to_all x3 -> x6, waiting for transfers between devices: 26.3 us -> 129 us  [exchange(): return lax.all_to_all(values, axis, split_axis=0, concat_axis=0, tiled=True)]
    psum x1 -> x0, blocking collectives: 40.1 us -> none  [shards(): totals = lax.psum((slices[0], slices[1], slices[2]), 'groups')]
    all_to_all x3 -> x6, starting transfers between devices: 29.4 us -> 67.5 us  [exchange(): return lax.all_to_all(values, axis, split_axis=0, concat_axis=0, tiled=True)]
    unnamed x6 -> x0, waiting for transfers between devices: 37.9 us -> none
    gather x2 -> x0, local copies, waits for them, and re-layouts: 33.7 us -> none  [the longest x1 20.7 us: shards(): next_emb = looked[next_dest, next_slot].reshape(samples, -1)]
    unnamed x35 -> x36, local copies, waits for them, and re-layouts: 34.1 us -> 1.96 us
  transfers between devices with their start and end apart: 8 -> 6, of which waited for: 6 -> 6; matrix products, arithmetic and copies ran while one was open for 5% -> 16% of each run, Pallas kernels for 0% -> 0%
where the time goes in v1:
time: 262 us; the launch traced here: 260 us
  waiting for transfers between devices  129 us (49%)
  starting transfers between devices  67.5 us (26%)
  matrix products  35.7 us (14%)
  local copies, waits for them, and re-layouts  16.5 us (6%)
  other arithmetic  10.6 us (4%)
    all_to_all x6, waiting for transfers between devices, exchange(): return lax.all_to_all(values, axis, split_axis=0, concat_axis=0, tiled=True)  129 us
    all_to_all x6, starting transfers between devices, exchange(): return lax.all_to_all(values, axis, split_axis=0, concat_axis=0, tiled=True)  67.5 us
    concatenate x4, local copies, waits for them, and re-layouts, shards(): jnp.concatenate([grad_in, grad_out, grad_bias[None], grad_head[None], jnp...  9.8 us
    dot_general x2, matrix products, asks(): found = jnp.dot(pick, digits, preferred_element_type=full)  8.45 us
    dot_general x1, matrix products, shards(): lax.dot_general(next_pick, looked, (((0,), (0,)), ((), ())), preferred_el...  8.13 us
    dot_general x1, matrix products, shards(): jnp.dot(prev_pick, grads, preferred_element_type=full).astype(half)  5.68 us
  transfers between devices with their start and end apart: 6, of which 6 were waited for; matrix products, arithmetic and copies ran while one was open for 16% of the time, Pallas kernels for 0%

profile of v1, /device:TPU:1, one launch (start us, length us, event | category | flops | bytes accessed | tf_op | source)
XLA Modules:
  0.0 260.4 jit_solution(9807454691407659489)
XLA Ops:
  0.7 0.9 convert_reduce_fusion.1
  1.6 1.0 fusion.28
  2.7 0.7 add_bitcast_fusion.1
  3.4 0.7 broadcast_add_fusion.1
  4.2 4.2 %fusion.3 = f32[3072,2]{0,1:T(2,128)S(1)} fusion(s32[2048]{0:T(1024)S(1)} %add_bitcast_fusion.1, bf16[2048,1]{0,1:T(2,128)(2,1)S(1)} %fusion.52, bf16[2048,1]{0,1:T(2,128)(2,1)S(1)} %get-tuple-element.10), kind=kOutput, calls=%fused_computation.5 | convolution fusion | flops 31473664 | bytes 40960 | tf_op jit(solution)/shard_map/dot_general | solution.py:66
  9.2 4.2 %fusion.1 = f32[3072,2]{0,1:T(2,128)S(1)} fusion(s32[2048]{0:T(1024)S(1)} %add_bitcast_fusion, bf16[2048,1]{0,1:T(2,128)(2,1)S(1)} %fusion.53, bf16[2048,1]{0,1:T(2,128)(2,1)S(1)} %get-tuple-element.12), kind=kOutput, calls=%fused_computation.2 | convolution fusion | flops 31473664 | bytes 40960 | tf_op jit(solution)/shard_map/dot_general | solution.py:66
  13.6 0.6 all_to_all.23
  14.2 10.7 %all-to-all-start = ((s32[32,1,192]{2,1,0:T(1,128)}), s32[32,1,192]{2,1,0:T(1,128)S(1)}, u32[]{:S(2)}, u32[]{:S(2)}) async-start(s32[32,1,192]{2,1,0:T(1,128)} %all_to_all.23), calls=%async_computation | async-start | bytes 65536 | tf_op jit(solution)/shard_map/all_to_all | solution.py:25
  24.9 0.7 copy.32
  25.6 0.5 copy.33
  26.2 5.7 %fusion.16 = bf16[3072,256]{1,0:T(8,128)(2,1)} fusion(bf16[2048,256]{1,0:T(8,128)(2,1)S(1)} %bitcast.88, s32[2048]{0:T(1024)S(1)} %add_bitcast_fusion), kind=kOutput, calls=%fused_computation.23 | convolution fusion | flops 3228303360 | bytes 2629632 | tf_op jit(solution)/shard_map/dot_general | solution.py:79
  31.8 1.7 all-to-all-done
  33.5 7.8 %all-to-all-start.2 = ((bf16[32,96,256]{2,1,0:T(8,128)(2,1)}), bf16[32,96,256]{2,1,0:T(8,128)(2,1)}, u32[]{:S(2)}, u32[]{:S(2)}) async-start(bf16[32,96,256]{2,1,0:T(8,128)(2,1)} %bitcast.85), calls=%async_computation.2 | async-start | bytes 3145728 | tf_op jit(solution)/shard_map/all_to_all | solution.py:25
  41.4 0.4 convolution_convert_fusion.3
  41.8 0.7 multiply_reduce_fusion.1
  42.6 0.4 multiply_reduce_fusion
  43.1 0.4 fusion.69
  43.4 0.4 copy-done.2
  43.9 0.5 convolution_convert_fusion.2
  44.4 0.5 fusion.19
  44.9 0.5 fusion.20
  45.4 0.6 copy_bitcast_fusion
  46.0 9.2 %concatenate.25 = bf16[288,32,128]{2,0,1:T(8,128)(2,1)} concatenate(bf16[128,32,128]{2,0,1:T(8,128)(2,1)S(1)} %get-tuple-element.25, bf16[128,32,128]{2,0,1:T(8,128)(2,1)S(1)} %get-tuple-element.24, bf16[1,32,128]{2,0,1:T(2,128)(2,1)S(1)} %copy.36, bf16[1,32,128]{2,0,1:T(2,128)(2,1)S(1)} %copy.37, bf16[30,32,128]{2,0,1:T(8,128)(2,1)S(1)} %broadcast_in_dim.10), dimensions={0} | concatenate | bytes 4718592 | tf_op jit(solution)/shard_map/concatenate | solution.py:103
  55.2 17.1 %all-to-all-done.2 = bf16[32,96,256]{2,1,0:T(8,128)(2,1)} async-done(((bf16[32,96,256]{2,1,0:T(8,128)(2,1)}), bf16[32,96,256]{2,1,0:T(8,128)(2,1)}, u32[]{:S(2)}, u32[]{:S(2)}) %all-to-all-start.2) | async-done | bytes 1572896 | tf_op jit(solution)/shard_map/all_to_all | solution.py:25
  72.3 9.5 %all-to-all-start.3 = ((bf16[32,288,128]{2,1,0:T(8,128)(2,1)}), bf16[32,288,128]{2,1,0:T(8,128)(2,1)S(1)}, u32[]{:S(2)}, u32[]{:S(2)}) async-start(bf16[32,288,128]{2,1,0:T(8,128)(2,1)} %bitcast.29), calls=%async_computation.3 | async-start | bytes 4718592 | tf_op jit(solution)/shard_map/all_to_all | solution.py:25
  81.9 0.6 multiply_add_fusion.1
  82.6 3.6 %fusion.21 = bf16[24,32,256]{2,1,0:T(8,128)(2,1)} fusion(bf16[3072,256,1]{1,0,2:T(8,128)(2,1)} %bitcast.26, s32[3072]{0:T(1024)S(1)} %eq.122, s32[24,32]{1,0:T(8,128)} %multiply_add_fusion.1), kind=kOutput, calls=%fused_computation.33 | convolution fusion | flops 1210515456 | bytes 1981440 | tf_op jit(solution)/shard_map/dot_general | solution.py:120
  86.3 47.2 %all-to-all-done.3 = bf16[32,288,128]{2,1,0:T(8,128)(2,1)S(1)} async-done(((bf16[32,288,128]{2,1,0:T(8,128)(2,1)}), bf16[32,288,128]{2,1,0:T(8,128)(2,1)S(1)}, u32[]{:S(2)}, u32[]{:S(2)}) %all-to-all-start.3) | async-done | bytes 2359328 | tf_op jit(solution)/shard_map/all_to_all | solution.py:25
  133.4 0.3 reduce.3
  133.8 1.9 pad_maximum_fusion
  135.7 23.9 %all-to-all-start.4 = ((bf16[24,38,256]{2,1,0:T(8,128)(2,1)}), bf16[24,38,256]{2,1,0:T(8,128)(2,1)S(1)}, u32[]{:S(2)}, u32[]{:S(2)}) async-start(bf16[24,38,256]{2,1,0:T(8,128)(2,1)} %pad_maximum_fusion), calls=%async_computation.4 | async-start | bytes 983040 | tf_op jit(solution)/shard_map/all_to_all | solution.py:25
  159.6 3.1 %fusion.15 = bf16[3072,256]{1,0:T(8,128)(2,1)} fusion(s32[3072]{0:T(1024)S(1)} %eq.114, f32[768,256]{1,0:T(8,128)S(1)} %copy-done.7), kind=kOutput, calls=%fused_computation.22 | convolution fusion | flops 1211301888 | bytes 2371584 | tf_op jit(solution)/shard_map/dot_general | solution.py:111
  162.8 18.2 %all-to-all-done.4 = bf16[24,38,256]{2,1,0:T(8,128)(2,1)S(1)} async-done(((bf16[24,38,256]{2,1,0:T(8,128)(2,1)}), bf16[24,38,256]{2,1,0:T(8,128)(2,1)S(1)}, u32[]{:S(2)}, u32[]{:S(2)}) %all-to-all-start.4) | async-done | bytes 466976 | tf_op jit(solution)/shard_map/all_to_all | solution.py:25
  181.0 0.8 copy-done.5
  181.8 6.3 %all-to-all-start.1 = ((bf16[32,96,256]{2,1,0:T(8,128)(2,1)}), bf16[32,96,256]{2,1,0:T(8,128)(2,1)}, u32[]{:S(2)}, u32[]{:S(2)}) async-start(bf16[32,96,256]{2,1,0:T(8,128)(2,1)} %bitcast.86), calls=%async_computation.1 | async-start | bytes 3145728 | tf_op jit(solution)/shard_map/all_to_all | solution.py:25
  188.1 1.1 reduce_sum.101
  189.2 35.3 %all-to-all-done.1 = bf16[32,96,256]{2,1,0:T(8,128)(2,1)} async-done(((bf16[32,96,256]{2,1,0:T(8,128)(2,1)}), bf16[32,96,256]{2,1,0:T(8,128)(2,1)}, u32[]{:S(2)}, u32[]{:S(2)}) %all-to-all-start.1) | async-done | bytes 1572896 | tf_op jit(solution)/shard_map/all_to_all | solution.py:25
  224.5 0.8 broadcast_in_dim.11
  225.3 9.3 %all-to-all-start.5 = ((bf16[24,38,256]{2,1,0:T(8,128)(2,1)}), bf16[24,38,256]{2,1,0:T(8,128)(2,1)}, u32[]{:S(2)}, u32[]{:S(2)}) async-start(bf16[24,38,256]{2,1,0:T(8,128)(2,1)} %broadcast_in_dim.11), calls=%async_computation.5 | async-start | bytes 983040 | tf_op jit(solution)/shard_map/all_to_all | solution.py:25
  234.7 2.7 %fusion.11 = bf16[128,4096]{1,0:T(8,128)(2,1)} fusion(bf16[128,128]{1,0:T(8,128)(2,1)S(1)} %convolution_convert_fusion.2, bf16[128,4096]{1,0:T(8,128)(2,1)} %param.22, f32[128,4096]{1,0:T(8,128)S(1)} %copy-done.3, f32[128]{0:T(128)S(1)} %copy-done.14, f32[4096]{0:T(1024)S(1)} %convert_element_type.96), kind=kOutput, calls=%fused_computation.16 | convolution fusion | flops 136839168 | bytes 4243968 | tf_op jit(solution)/shard_map/dot_general | solution.py:95
  237.4 8.1 %fusion.17 = bf16[2048,256]{1,0:T(8,128)(2,1)S(1)} fusion(bf16[3072,256]{1,0:T(8,128)(2,1)} %bitcast.18, s32[2048]{0:T(1024)S(1)} %add_bitcast_fusion.1), kind=kOutput, calls=%fused_computation.27 | convolution fusion | flops 3228041216 | bytes 2629632 | tf_op jit(solution)/shard_map/dot_general | solution.py:115
  245.5 1.1 copy.41
  246.6 9.6 %all-to-all-done.5 = bf16[24,38,256]{2,1,0:T(8,128)(2,1)} async-done(((bf16[24,38,256]{2,1,0:T(8,128)(2,1)}), bf16[24,38,256]{2,1,0:T(8,128)(2,1)}, u32[]{:S(2)}, u32[]{:S(2)}) %all-to-all-start.5) | async-done | bytes 466976 | tf_op jit(solution)/shard_map/all_to_all | solution.py:25
  256.1 1.1 convert_element_type.104
  257.5 0.7 fusion.72
  258.1 0.5 slice_bitcast_fusion
  258.7 0.6 sqrt_add_fusion
  259.3 1.1 fusion.30
  (65 shorter events, 1.7 us)
Async XLA Ops:
  0.6 41.2 %copy-start = (bf16[128,4096]{1,0:T(8,128)(2,1)S(1)}, bf16[128,4096]{1,0:T(8,128)(2,1)}, u32[]{:S(2)}) copy-start(bf16[128,4096]{1,0:T(8,128)(2,1)} %param.23) | copy-start | bytes 3145732
  4.2 4.4 %copy-start.9 = (s32[128,16,1]{0,2,1:T(1,128)S(1)}, s32[128,16,1]{0,2,1:T(1,128)}, u32[]{:S(2)}) copy-start(s32[128,16,1]{0,2,1:T(1,128)} %param.15) | copy-start | bytes 24580
  4.2 4.9 %copy-start.12 = (s32[128,16]{0,1:T(8,128)S(1)}, s32[128,16]{0,1:T(8,128)}, u32[]{:S(2)}) copy-start(s32[128,16]{0,1:T(8,128)} %param.16) | copy-start | bytes 24580
  9.2 15.8 %copy-start.6 = (bf16[128,4096]{1,0:T(8,128)(2,1)S(1)}, bf16[128,4096]{1,0:T(8,128)(2,1)}, u32[]{:S(2)}) copy-start(bf16[128,4096]{1,0:T(8,128)(2,1)} %param.18) | copy-start | bytes 3145732
  14.2 19.3 %all-to-all-start = ((s32[32,1,192]{2,1,0:T(1,128)}), s32[32,1,192]{2,1,0:T(1,128)S(1)}, u32[]{:S(2)}, u32[]{:S(2)}) async-start(s32[32,1,192]{2,1,0:T(1,128)} %all_to_all.23), calls=%async_computation | async-start | bytes 65536 | tf_op jit(solution)/shard_map/all_to_all | solution.py:25
  31.8 9.5 %copy-start.11 = (bf16[4096]{0:T(1024)(128)(2,1)S(1)}, bf16[4096]{0:T(1024)(128)(2,1)}, u32[]{:S(2)}) copy-start(bf16[4096]{0:T(1024)(128)(2,1)} %param.25) | copy-start | bytes 24580
  31.8 9.5 %copy-start.1 = (bf16[128,4096]{1,0:T(8,128)(2,1)S(1)}, bf16[128,4096]{1,0:T(8,128)(2,1)}, u32[]{:S(2)}) copy-start(bf16[128,4096]{1,0:T(8,128)(2,1)} %param.17) | copy-start | bytes 3145732
  31.8 9.5 %copy-start.4 = (bf16[128,4096]{1,0:T(8,128)(2,1)S(1)}, bf16[128,4096]{1,0:T(8,128)(2,1)}, u32[]{:S(2)}) copy-start(bf16[128,4096]{1,0:T(8,128)(2,1)} %param.22) | copy-start | bytes 3145732
  33.5 8.3 %copy-start.10 = (f32[4096]{0:T(1024)S(1)}, f32[4096]{0:T(1024)}, u32[]{:S(2)}) copy-start(f32[4096]{0:T(1024)} %param.24) | copy-start | bytes 49156
  33.5 38.8 %all-to-all-start.2 = ((bf16[32,96,256]{2,1,0:T(8,128)(2,1)}), bf16[32,96,256]{2,1,0:T(8,128)(2,1)}, u32[]{:S(2)}, u32[]{:S(2)}) async-start(bf16[32,96,256]{2,1,0:T(8,128)(2,1)} %bitcast.85), calls=%async_computation.2 | async-start | bytes 3145728 | tf_op jit(solution)/shard_map/all_to_all | solution.py:25
  41.8 0.7 copy-start.16
  42.6 1.3 copy-start.2
  42.6 2.3 copy-start.13
  72.3 61.1 %all-to-all-start.3 = ((bf16[32,288,128]{2,1,0:T(8,128)(2,1)}), bf16[32,288,128]{2,1,0:T(8,128)(2,1)S(1)}, u32[]{:S(2)}, u32[]{:S(2)}) async-start(bf16[32,288,128]{2,1,0:T(8,128)(2,1)} %bitcast.29), calls=%async_computation.3 | async-start | bytes 4718592 | tf_op jit(solution)/shard_map/all_to_all | solution.py:25
  133.8 25.9 %copy-start.7 = (f32[768,256]{1,0:T(8,128)S(1)}, f32[768,256]{1,0:T(8,128)}, u32[]{:S(2)}) copy-start(f32[768,256]{1,0:T(8,128)} %param.20) | copy-start | bytes 2359300
  135.7 45.3 %all-to-all-start.4 = ((bf16[24,38,256]{2,1,0:T(8,128)(2,1)}), bf16[24,38,256]{2,1,0:T(8,128)(2,1)S(1)}, u32[]{:S(2)}, u32[]{:S(2)}) async-start(bf16[24,38,256]{2,1,0:T(8,128)(2,1)} %pad_maximum_fusion), calls=%async_computation.4 | async-start | bytes 983040 | tf_op jit(solution)/shard_map/all_to_all | solution.py:25
  181.0 0.8 copy-start.5
  181.8 52.9 %copy-start.3 = (f32[128,4096]{1,0:T(8,128)S(1)}, f32[128,4096]{1,0:T(8,128)}, u32[]{:S(2)}) copy-start(f32[128,4096]{1,0:T(8,128)} %copy-done.2) | copy-start | bytes 6291460
  181.8 52.9 %copy-start.14 = (f32[128]{0:T(128)S(1)}, f32[128]{0:T(128)}, u32[]{:S(2)}) copy-start(f32[128]{0:T(128)} %copy-done.13) | copy-start | bytes 1540
  181.8 42.8 %all-to-all-start.1 = ((bf16[32,96,256]{2,1,0:T(8,128)(2,1)}), bf16[32,96,256]{2,1,0:T(8,128)(2,1)}, u32[]{:S(2)}, u32[]{:S(2)}) async-start(bf16[32,96,256]{2,1,0:T(8,128)(2,1)} %bitcast.86), calls=%async_computation.1 | async-start | bytes 3145728 | tf_op jit(solution)/shard_map/all_to_all | solution.py:25
  225.3 30.8 %all-to-all-start.5 = ((bf16[24,38,256]{2,1,0:T(8,128)(2,1)}), bf16[24,38,256]{2,1,0:T(8,128)(2,1)}, u32[]{:S(2)}, u32[]{:S(2)}) async-start(bf16[24,38,256]{2,1,0:T(8,128)(2,1)} %broadcast_in_dim.11), calls=%async_computation.5 | async-start | bytes 983040 | tf_op jit(solution)/shard_map/all_to_all | solution.py:25
  246.6 12.2 %copy-start.15 = (f32[768]{0:T(1024)S(1)}, f32[768]{0:T(1024)}, u32[]{:S(2)}) copy-start(f32[768]{0:T(1024)} %param.21) | copy-start | bytes 9220
  246.6 12.8 %copy-start.8 = (f32[768,256]{1,0:T(8,128)S(1)}, f32[768,256]{1,0:T(8,128)}, u32[]{:S(2)}) copy-start(f32[768,256]{1,0:T(8,128)} %param.20) | copy-start | bytes 2359300
